TPU v7x, 512 devices: a whole 4x4x16 slice. The times are simulated.
512 devices in a mesh: ctx: 128 (over z, y, core), head: 4 (over x).
Axes of the slice: x: 4, y: 4, z: 16, core: 2. Of those that a mesh axis runs over, the one named last changes fastest.
Arguments:
- queries: bfloat16 [16384, 4096], P(('ctx', 'head')), may hold values from -24 to 24
- key_rows: bfloat16 [16384, 4096], P(('ctx', 'head')), may hold values from -12 to 12
- value_rows: bfloat16 [16384, 4096], P(('ctx', 'head')), may hold values from -6 to 6
- rel_bias: float32 [32, 32], P(None, 'head'), may hold values from -4 to 4
- offsets: int32 [2, 32], P(None, 'head'), may hold values from 0 to 63, as said below
Outputs:
- attended: bfloat16 [16384, 4096], P(('ctx', 'head'))
Inputs may be any that keep to these rules, and one draw needn't show every extreme that they name: offsets[0, h] is below 4 and offsets[1, h] is below 64.
All inputs are finite; a program needn't handle non-finite values.
Results may differ from a plain program's by a relative error of at most 0.005.
Values may be sent and summed in bfloat16 or wider, within the bound.
No kernel may reach another device: no remote copies, remote signals or barrier semaphores. Data moves between devices by JAX's collectives and lax.ppermute only.
A program may use at most 64 MiB of HBM per device.

v0:
```python
import math
import jax
import jax.numpy as jnp
from jax import lax
from jax.sharding import PartitionSpec as P

DH = 128
BUCKETS = 32
MAXDIST = 128
R1 = 4
SPAN = 256


def shifted(block, axis, distance):
    devices = range(lax.axis_size(axis))
    route = [(i - distance, i) for i in devices if i - distance in devices]
    return lax.ppermute(block, axis, route)


def bucket_edges():
    half_count = BUCKETS // 2
    thresholds = []
    for target in range(half_count + 1, BUCKETS):
        thresholds.append(
            int(
                math.ceil(
                    half_count * (MAXDIST / half_count) ** ((target - half_count) / half_count)
                )
            )
        )
    return thresholds


def bucket_of(token_separation):
    half_count = BUCKETS // 2
    far_bucket = jnp.full(token_separation.shape, half_count, jnp.int32)
    for border in bucket_edges():
        far_bucket = far_bucket + (token_separation >= border).astype(jnp.int32)
    return jnp.where(token_separation < half_count, token_separation, far_bucket)


def bias_block(position_bias_lookup, ask_count, key_count, advance, stride):
    ask_spots = jnp.arange(ask_count, dtype=jnp.int32)[:, None]
    key_spots = jnp.arange(key_count, dtype=jnp.int32)[None, :]
    token_separation = jnp.maximum((ask_spots - key_spots + advance) * stride, 0)
    bucket_grid = bucket_of(token_separation)
    indicator_matrix = (
        jnp.arange(BUCKETS, dtype=jnp.int32)[:, None, None] == bucket_grid[None]
    ).astype(jnp.float32)
    return jnp.einsum(
        "lnd,lc->cnd", indicator_matrix, position_bias_lookup, precision=lax.Precision.HIGHEST
    )


def start_state(ask_count, n_heads):
    return (
        jnp.full((n_heads, ask_count), -1e30, jnp.float32),
        jnp.zeros((n_heads, ask_count), jnp.float32),
        jnp.zeros((ask_count, n_heads, DH), jnp.float32),
    )


def attend(running, asks, key_part, value_part, advance, stride, position_bias_lookup, usable):
    ask_count = asks.shape[0]
    key_count = key_part.shape[0]
    scores = jnp.einsum(
        "qhd,khd->hqk", asks, key_part, preferred_element_type=jnp.float32
    ) * asks.shape[2] ** (-0.5)
    scores = scores + bias_block(position_bias_lookup, ask_count, key_count, advance, stride)
    allowed = (
        jnp.arange(ask_count, dtype=jnp.int32)[:, None] + advance
        >= jnp.arange(key_count, dtype=jnp.int32)[None, :]
    ) & usable
    held = jnp.where(allowed[None], scores, -1e30)
    row_top, row_sum, row_acc = running
    fresh = jnp.maximum(row_top, jnp.max(held, axis=2))
    weights = jnp.where(allowed[None], jnp.exp(held - fresh[:, :, None]), 0.0)
    shrink = jnp.exp(row_top - fresh)
    row_sum = row_sum * shrink + jnp.sum(weights, axis=2)
    blended = jnp.einsum(
        "hqk,khd->qhd", weights.astype(jnp.bfloat16), value_part, preferred_element_type=jnp.float32
    )
    row_acc = row_acc * jnp.transpose(shrink)[:, :, None] + blended
    return (fresh, row_sum, row_acc)


def finish(running):
    row_top, row_sum, row_acc = running
    result = (row_acc / jnp.transpose(row_sum)[:, :, None]).astype(jnp.bfloat16)
    return (result, jnp.transpose(row_top + jnp.log(row_sum)))


def select_rows(tokens, picks, stride):
    n_rows, n_heads, head_dim = tokens.shape
    grouped = tokens.reshape(n_rows // stride, stride, n_heads, head_dim)
    wanted = jnp.arange(stride, dtype=jnp.int32)[None, :, None, None] == picks[None, None, :, None]
    picked = jnp.where(wanted, grouped, jnp.zeros((), tokens.dtype))
    return jnp.sum(picked, axis=1, dtype=tokens.dtype)


def merge_block(
    first_out, leading_logsumexp, mid_out, mid_lse, far_out, far_lse, mid_pick, far_pick
):
    long_rate = first_out.shape[1]
    spots = jnp.arange(long_rate, dtype=jnp.int32)[:, None]
    mid_cover = (spots % R1 == mid_pick[None, :])[None]
    far_cover = (spots == far_pick[None, :])[None]
    mid_lse_wide = jnp.repeat(mid_lse, R1, axis=1)
    mid_out_wide = jnp.repeat(mid_out, R1, axis=1)
    far_lse_wide = jnp.broadcast_to(far_lse[:, None, :], leading_logsumexp.shape)
    peak = jnp.maximum(
        leading_logsumexp,
        jnp.maximum(
            jnp.where(mid_cover, mid_lse_wide, leading_logsumexp),
            jnp.where(far_cover, far_lse_wide, leading_logsumexp),
        ),
    )
    first_weight = jnp.exp(leading_logsumexp - peak)
    mid_weight = jnp.where(mid_cover, jnp.exp(jnp.where(mid_cover, mid_lse_wide, peak) - peak), 0.0)
    far_weight = jnp.where(far_cover, jnp.exp(jnp.where(far_cover, far_lse_wide, peak) - peak), 0.0)
    blended = (
        first_weight[..., None] * first_out.astype(jnp.float32)
        + mid_weight[..., None] * mid_out_wide.astype(jnp.float32)
        + far_weight[..., None] * far_out[:, None].astype(jnp.float32)
    )
    return (blended / (first_weight + mid_weight + far_weight)[..., None]).astype(jnp.bfloat16)


def nearby_dilation_period(running, asks, moving, kept, position_bias_lookup, position, group):
    tok_rows = asks.shape[0]

    def near_turn(turn_no, carried):
        current_state_value, moving_now, kept_now = carried
        moving_now = shifted(moving_now, "ctx", 1)
        current_state_value = attend(
            current_state_value,
            asks,
            moving_now[0],
            moving_now[1],
            turn_no * tok_rows,
            1,
            position_bias_lookup,
            position >= turn_no,
        )
        return (current_state_value, moving_now, kept_now)

    result = lax.fori_loop(1, group, near_turn, (running, moving, kept))
    return (result[0], result[2])


def mid_cycle(running, asks, moving, position_bias_lookup, position, from_turn, group):
    mid_rows = asks.shape[0]

    def mid_turn(turn_no, carried):
        current_state_value, moving_now = carried
        moving_now = shifted(moving_now, "ctx", 1)
        current_state_value = attend(
            current_state_value,
            asks,
            moving_now[0],
            moving_now[1],
            turn_no * mid_rows,
            R1,
            position_bias_lookup,
            position >= turn_no,
        )
        return (current_state_value, moving_now)

    return lax.fori_loop(from_turn, group, mid_turn, (running, moving))[0]


def on_device(queries, key_rows, value_rows, rel_bias, offsets):
    local_q, local_k, local_v = (
        lax.all_to_all(queries, "head", split_axis=1, concat_axis=0, tiled=True),
        lax.all_to_all(key_rows, "head", split_axis=1, concat_axis=0, tiled=True),
        lax.all_to_all(value_rows, "head", split_axis=1, concat_axis=0, tiled=True),
    )
    tok_rows = local_q.shape[0]
    n_heads = rel_bias.shape[1]
    asks = local_q.reshape(tok_rows, n_heads, DH)
    keys_here = local_k.reshape(tok_rows, n_heads, DH)
    vals_here = local_v.reshape(tok_rows, n_heads, DH)
    n_ctx = lax.axis_size("ctx")
    place = lax.axis_index("ctx")
    long_rate = tok_rows * n_ctx // SPAN
    near_group = SPAN // tok_rows
    mid_rows = tok_rows // R1
    mid_group = R1 * SPAN // tok_rows
    far_rows = tok_rows // long_rate
    mid_pick = offsets[0]
    far_pick = offsets[1]
    mid_q = select_rows(asks, mid_pick, R1)
    mid_k = select_rows(keys_here, mid_pick, R1)
    mid_v = select_rows(vals_here, mid_pick, R1)
    mid_pair = jnp.stack([mid_k, mid_v])
    first_state = attend(
        start_state(tok_rows, n_heads), asks, keys_here, vals_here, 0, 1, rel_bias, True
    )
    first_state, kept = nearby_dilation_period(
        first_state,
        asks,
        jnp.stack([keys_here, vals_here]),
        mid_pair,
        rel_bias,
        place % near_group,
        near_group,
    )
    mid_state = attend(start_state(mid_rows, n_heads), mid_q, mid_k, mid_v, 0, R1, rel_bias, True)
    mid_state = mid_cycle(mid_state, mid_q, mid_pair, rel_bias, place % mid_group, 1, mid_group)
    far_q = select_rows(asks, far_pick, long_rate)
    far_k = select_rows(keys_here, far_pick, long_rate)
    far_v = select_rows(vals_here, far_pick, long_rate)
    far_state = attend(
        start_state(far_rows, n_heads),
        far_q,
        lax.all_gather(far_k, "ctx", axis=0, tiled=True),
        lax.all_gather(far_v, "ctx", axis=0, tiled=True),
        place * far_rows,
        long_rate,
        rel_bias,
        True,
    )
    far_out, far_lse = finish(far_state)
    first_out, leading_logsumexp = finish(first_state)
    mid_out, mid_lse = finish(mid_state)
    merged = merge_block(
        first_out.reshape(far_rows, long_rate, n_heads, DH),
        leading_logsumexp.reshape(far_rows, long_rate, n_heads),
        mid_out.reshape(far_rows, long_rate // R1, n_heads, DH),
        mid_lse.reshape(far_rows, long_rate // R1, n_heads),
        far_out,
        far_lse,
        mid_pick,
        far_pick,
    )
    merged = merged.reshape(tok_rows, n_heads * DH)
    return lax.all_to_all(merged, "head", split_axis=0, concat_axis=1, tiled=True)


def solution(mesh):
    in_specs = (
        P(("ctx", "head"), None),
        P(("ctx", "head"), None),
        P(("ctx", "head"), None),
        P(None, "head"),
        P(None, "head"),
    )
    out_specs = P(("ctx", "head"), None)
    return jax.shard_map(
        on_device, mesh=mesh, in_specs=in_specs, out_specs=out_specs, check_vma=False
    )
```

profile of v0, /device:TPU:128, one launch (start us, length us, event | category | flops | bytes accessed | tf_op | source)
XLA Modules:
  0.0 295.4 jit_solution(1167431653436418967)
XLA Ops:
  0.0 1.7 copy.297
  1.7 4.3 %all-to-all-start = ((bf16[32,4,1024]{2,0,1:T(8,128)(2,1)}), bf16[32,4,1024]{2,0,1:T(8,128)(2,1)S(1)}, u32[]{:S(2)}, u32[]{:S(2)}) async-start(bf16[32,4,1024]{2,0,1:T(8,128)(2,1)} %bitcast.228), calls=%async_computation | async-start | bytes 524288 | tf_op jit(solution)/shard_map/all_to_all | solution.py:174
  6.5 0.3 fusion.53
  7.3 0.7 copy.296
  8.0 0.7 copy.295
  8.7 0.7 fusion.31
  9.4 0.2 copy.204
  9.7 0.7 fusion.30
  10.4 0.2 copy.199
  10.7 2.0 all-to-all-done
  12.7 3.4 %all-to-all-start.1 = ((bf16[32,4,1024]{2,0,1:T(8,128)(2,1)}), bf16[32,4,1024]{2,0,1:T(8,128)(2,1)S(1)}, u32[]{:S(2)}, u32[]{:S(2)}) async-start(bf16[32,4,1024]{2,0,1:T(8,128)(2,1)} %bitcast.227), calls=%async_computation.1 | async-start | bytes 524288 | tf_op jit(solution)/shard_map/all_to_all | solution.py:175
  16.1 6.6 %all-to-all-done.1 = bf16[32,4,1024]{2,0,1:T(8,128)(2,1)S(1)} async-done(((bf16[32,4,1024]{2,0,1:T(8,128)(2,1)}), bf16[32,4,1024]{2,0,1:T(8,128)(2,1)S(1)}, u32[]{:S(2)}, u32[]{:S(2)}) %all-to-all-start.1) | async-done | bytes 262176 | tf_op jit(solution)/shard_map/all_to_all | solution.py:175
  22.7 3.4 %all-to-all-start.2 = ((bf16[32,4,1024]{2,0,1:T(8,128)(2,1)}), bf16[32,4,1024]{2,0,1:T(8,128)(2,1)S(1)}, u32[]{:S(2)}, u32[]{:S(2)}) async-start(bf16[32,4,1024]{2,0,1:T(8,128)(2,1)} %bitcast.226), calls=%async_computation.2 | async-start | bytes 524288 | tf_op jit(solution)/shard_map/all_to_all | solution.py:176
  26.3 6.5 %all-to-all-done.2 = bf16[32,4,1024]{2,0,1:T(8,128)(2,1)S(1)} async-done(((bf16[32,4,1024]{2,0,1:T(8,128)(2,1)}), bf16[32,4,1024]{2,0,1:T(8,128)(2,1)S(1)}, u32[]{:S(2)}, u32[]{:S(2)}) %all-to-all-start.2) | async-done | bytes 262176 | tf_op jit(solution)/shard_map/all_to_all | solution.py:176
  32.8 0.2 fusion.60
  33.2 0.3 select_reduce_fusion
  33.8 0.2 fusion.43
  34.1 85.1 %all_gather.6 = bf16[256,8,128]{2,1,0:T(8,128)(2,1)S(1)} all-gather(bf16[2,8,128]{2,1,0:T(8,128)(2,1)S(1)} %reduce_sum.144), channel_id=1, replica_groups=mesh['ctx'=128,'head'=4] {'ctx'}, dimensions={0}, use_global_device_ids=true | all-gather | bytes 528384 | tf_op jit(solution)/shard_map/all_gather | solution.py:216
  119.2 0.3 fusion.180
  119.7 80.7 %all_gather.7 = bf16[256,8,128]{2,1,0:T(8,128)(2,1)S(1)} all-gather(bf16[2,8,128]{2,1,0:T(8,128)(2,1)S(1)} %reduce_sum.149), channel_id=1, replica_groups=mesh['ctx'=128,'head'=4] {'ctx'}, dimensions={0}, use_global_device_ids=true | all-gather | bytes 528384 | tf_op jit(solution)/shard_map/all_gather | solution.py:217
  200.4 0.2 fusion.50
  200.7 2.4 collective-permute-start.1
  203.2 74.2 %while.4 = (s32[]{:T(128)}, f32[8,32]{1,0:T(8,128)S(1)}, f32[8,32]{1,0:T(8,128)S(1)}, f32[32,8,128]{2,0,1:T(8,128)S(1)}, bf16[2,32,8,128]{3,1,2,0:T(8,128)(2,1)S...) while((s32[]{:T(128)}, f32[8,32]{1,0:T(8,128)S(1)}, ...), condition=%wide.region_12.13_spmd, body=%wide.region_9.12_spmd.sunk | while | flops 7575332 | bytes 1713579 | solution.py:169
  203.2 2.6 collective-permute-start
  205.9 0.3 fusion.194
  206.3 9.7 %collective-permute-done = bf16[2,32,8,128]{3,1,2,0:T(8,128)(2,1)S(1)} collective-permute-done((bf16[2,32,8,128]{3,1,2,0:T(8,128)(2,1)S(1)}, bf16[2,32,8,128]{3,1,2,0:T(8,128)(2,1)S(1)}, u32[]{:S(2)}, u32[]{:S(2)}) %collective-permute-start) | collective-permute-done | bytes 131104 | tf_op jit(solution)/shard_map/while/body/eval_jaxpr/ppermute | solution.py:17
  216.3 0.2 fusion.199
  216.5 1.9 collective-permute-start
  218.5 0.3 fusion.194
  218.9 7.2 %collective-permute-done = bf16[2,32,8,128]{3,1,2,0:T(8,128)(2,1)S(1)} collective-permute-done((bf16[2,32,8,128]{3,1,2,0:T(8,128)(2,1)S(1)}, bf16[2,32,8,128]{3,1,2,0:T(8,128)(2,1)S(1)}, u32[]{:S(2)}, u32[]{:S(2)}) %collective-permute-start) | collective-permute-done | bytes 131104 | tf_op jit(solution)/shard_map/while/body/eval_jaxpr/ppermute | solution.py:17
  226.4 0.2 fusion.199
  226.7 1.9 collective-permute-start
  228.6 0.3 fusion.194
  229.0 7.2 %collective-permute-done = bf16[2,32,8,128]{3,1,2,0:T(8,128)(2,1)S(1)} collective-permute-done((bf16[2,32,8,128]{3,1,2,0:T(8,128)(2,1)S(1)}, bf16[2,32,8,128]{3,1,2,0:T(8,128)(2,1)S(1)}, u32[]{:S(2)}, u32[]{:S(2)}) %collective-permute-start) | collective-permute-done | bytes 131104 | tf_op jit(solution)/shard_map/while/body/eval_jaxpr/ppermute | solution.py:17
  236.5 0.2 fusion.199
  236.8 1.9 collective-permute-start
  238.8 0.3 fusion.194
  239.2 7.2 %collective-permute-done = bf16[2,32,8,128]{3,1,2,0:T(8,128)(2,1)S(1)} collective-permute-done((bf16[2,32,8,128]{3,1,2,0:T(8,128)(2,1)S(1)}, bf16[2,32,8,128]{3,1,2,0:T(8,128)(2,1)S(1)}, u32[]{:S(2)}, u32[]{:S(2)}) %collective-permute-start) | collective-permute-done | bytes 131104 | tf_op jit(solution)/shard_map/while/body/eval_jaxpr/ppermute | solution.py:17
  246.7 0.2 fusion.199
  246.9 1.9 collective-permute-start
  248.9 0.3 fusion.194
  249.3 7.2 %collective-permute-done = bf16[2,32,8,128]{3,1,2,0:T(8,128)(2,1)S(1)} collective-permute-done((bf16[2,32,8,128]{3,1,2,0:T(8,128)(2,1)S(1)}, bf16[2,32,8,128]{3,1,2,0:T(8,128)(2,1)S(1)}, u32[]{:S(2)}, u32[]{:S(2)}) %collective-permute-start) | collective-permute-done | bytes 131104 | tf_op jit(solution)/shard_map/while/body/eval_jaxpr/ppermute | solution.py:17
  256.8 0.2 fusion.199
  257.1 1.9 collective-permute-start
  259.1 0.3 fusion.194
  259.5 7.2 %collective-permute-done = bf16[2,32,8,128]{3,1,2,0:T(8,128)(2,1)S(1)} collective-permute-done((bf16[2,32,8,128]{3,1,2,0:T(8,128)(2,1)S(1)}, bf16[2,32,8,128]{3,1,2,0:T(8,128)(2,1)S(1)}, u32[]{:S(2)}, u32[]{:S(2)}) %collective-permute-start) | collective-permute-done | bytes 131104 | tf_op jit(solution)/shard_map/while/body/eval_jaxpr/ppermute | solution.py:17
  267.0 0.2 fusion.199
  267.2 1.9 collective-permute-start
  269.2 0.3 fusion.194
  269.6 7.2 %collective-permute-done = bf16[2,32,8,128]{3,1,2,0:T(8,128)(2,1)S(1)} collective-permute-done((bf16[2,32,8,128]{3,1,2,0:T(8,128)(2,1)S(1)}, bf16[2,32,8,128]{3,1,2,0:T(8,128)(2,1)S(1)}, u32[]{:S(2)}, u32[]{:S(2)}) %collective-permute-start) | collective-permute-done | bytes 131104 | tf_op jit(solution)/shard_map/while/body/eval_jaxpr/ppermute | solution.py:17
  277.1 0.2 fusion.199
  278.1 0.3 fusion.179
  278.4 1.3 fusion.178
  279.7 0.2 fusion.55
  279.9 0.5 fusion.33
  280.4 1.3 fusion.42
  281.7 0.3 copy.223
  282.3 0.2 div.42
  282.6 0.2 mul.189
  282.9 0.2 mul.183
  283.4 0.9 mul.193
  284.3 1.3 divide_convert_fusion
  285.6 9.1 %all_to_all.64 = bf16[4,32,1024]{2,1,0:T(8,128)(2,1)S(1)} all-to-all(bf16[4,32,1024]{2,1,0:T(8,128)(2,1)S(1)} %divide_convert_fusion), channel_id=1, replica_groups=mesh['ctx'=128,'head'=4] {'head'}, dimensions={0} | all-to-all | bytes 524288 | tf_op jit(solution)/shard_map/all_to_all | solution.py:237
  294.7 0.7 copy.240
  (141 shorter events, 6.0 us)
Async XLA Ops:
  0.0 6.3 %copy-start.3 = (s32[2,8]{1,0:T(2,128)S(1)}, s32[2,8]{1,0:T(2,128)}, u32[]{:S(2)}) copy-start(s32[2,8]{1,0:T(2,128)} %param.11) | copy-start | bytes 196
  0.0 6.3 %copy-start = (f32[32,8]{0,1:T(8,128)S(1)}, f32[32,8]{0,1:T(8,128)}, u32[]{:S(2)}) copy-start(f32[32,8]{0,1:T(8,128)} %param.10) | copy-start | bytes 3076
  1.7 11.0 %all-to-all-start = ((bf16[32,4,1024]{2,0,1:T(8,128)(2,1)}), bf16[32,4,1024]{2,0,1:T(8,128)(2,1)S(1)}, u32[]{:S(2)}, u32[]{:S(2)}) async-start(bf16[32,4,1024]{2,0,1:T(8,128)(2,1)} %bitcast.228), calls=%async_computation | async-start | bytes 524288 | tf_op jit(solution)/shard_map/all_to_all | solution.py:174
  6.0 1.3 copy-start.1
  6.9 1.1 copy-start.2
  12.7 10.1 %all-to-all-start.1 = ((bf16[32,4,1024]{2,0,1:T(8,128)(2,1)}), bf16[32,4,1024]{2,0,1:T(8,128)(2,1)S(1)}, u32[]{:S(2)}, u32[]{:S(2)}) async-start(bf16[32,4,1024]{2,0,1:T(8,128)(2,1)} %bitcast.227), calls=%async_computation.1 | async-start | bytes 524288 | tf_op jit(solution)/shard_map/all_to_all | solution.py:175
  22.7 10.1 %all-to-all-start.2 = ((bf16[32,4,1024]{2,0,1:T(8,128)(2,1)}), bf16[32,4,1024]{2,0,1:T(8,128)(2,1)S(1)}, u32[]{:S(2)}, u32[]{:S(2)}) async-start(bf16[32,4,1024]{2,0,1:T(8,128)(2,1)} %bitcast.226), calls=%async_computation.2 | async-start | bytes 524288 | tf_op jit(solution)/shard_map/all_to_all | solution.py:176
  200.7 77.7 %collective-permute-start.1 = (bf16[2,128,8,128]{3,1,2,0:T(8,128)(2,1)S(1)}, bf16[2,128,8,128]{3,1,2,0:T(8,128)(2,1)}, u32[]{:S(2)}, u32[]{:S(2)}) collective-permute-start(bf16[2,128,8,128]{3,1,2,0:T(8,128)(2,1)S(1)} %pad_maximum_fusion), channel_id=1, source_target_pairs={{0,4},{4,8},{8,12},{12,16},{16,20},{20,24},{24,28},{28,32},{32,36}... | collective-permute-start | bytes 1572872 | tf_op jit(solution)/shard_map/while/body/eval_jaxpr/ppermute | solution.py:17
  203.2 12.8 %collective-permute-start = (bf16[2,32,8,128]{3,1,2,0:T(8,128)(2,1)S(1)}, bf16[2,32,8,128]{3,1,2,0:T(8,128)(2,1)S(1)}, u32[]{:S(2)}, u32[]{:S(2)}) collective-permute-start(bf16[2,32,8,128]{3,1,2,0:T(8,128)(2,1)S(1)} %get-tuple-element.334), channel_id=1, source_target_pairs={{0,4},{4,8},{8,12},{12,16},{16,20},{20,24},{24,28},{28,32},{32,36}... | collective-permute-start | bytes 393224 | tf_op jit(solution)/shard_map/while/body/eval_jaxpr/ppermute | solution.py:17
  216.5 9.6 %collective-permute-start = (bf16[2,32,8,128]{3,1,2,0:T(8,128)(2,1)S(1)}, bf16[2,32,8,128]{3,1,2,0:T(8,128)(2,1)S(1)}, u32[]{:S(2)}, u32[]{:S(2)}) collective-permute-start(bf16[2,32,8,128]{3,1,2,0:T(8,128)(2,1)S(1)} %get-tuple-element.334), channel_id=1, source_target_pairs={{0,4},{4,8},{8,12},{12,16},{16,20},{20,24},{24,28},{28,32},{32,36}... | collective-permute-start | bytes 393224 | tf_op jit(solution)/shard_map/while/body/eval_jaxpr/ppermute | solution.py:17
  226.7 9.6 %collective-permute-start = (bf16[2,32,8,128]{3,1,2,0:T(8,128)(2,1)S(1)}, bf16[2,32,8,128]{3,1,2,0:T(8,128)(2,1)S(1)}, u32[]{:S(2)}, u32[]{:S(2)}) collective-permute-start(bf16[2,32,8,128]{3,1,2,0:T(8,128)(2,1)S(1)} %get-tuple-element.334), channel_id=1, source_target_pairs={{0,4},{4,8},{8,12},{12,16},{16,20},{20,24},{24,28},{28,32},{32,36}... | collective-permute-start | bytes 393224 | tf_op jit(solution)/shard_map/while/body/eval_jaxpr/ppermute | solution.py:17
  236.8 9.6 %collective-permute-start = (bf16[2,32,8,128]{3,1,2,0:T(8,128)(2,1)S(1)}, bf16[2,32,8,128]{3,1,2,0:T(8,128)(2,1)S(1)}, u32[]{:S(2)}, u32[]{:S(2)}) collective-permute-start(bf16[2,32,8,128]{3,1,2,0:T(8,128)(2,1)S(1)} %get-tuple-element.334), channel_id=1, source_target_pairs={{0,4},{4,8},{8,12},{12,16},{16,20},{20,24},{24,28},{28,32},{32,36}... | collective-permute-start | bytes 393224 | tf_op jit(solution)/shard_map/while/body/eval_jaxpr/ppermute | solution.py:17
  246.9 9.6 %collective-permute-start = (bf16[2,32,8,128]{3,1,2,0:T(8,128)(2,1)S(1)}, bf16[2,32,8,128]{3,1,2,0:T(8,128)(2,1)S(1)}, u32[]{:S(2)}, u32[]{:S(2)}) collective-permute-start(bf16[2,32,8,128]{3,1,2,0:T(8,128)(2,1)S(1)} %get-tuple-element.334), channel_id=1, source_target_pairs={{0,4},{4,8},{8,12},{12,16},{16,20},{20,24},{24,28},{28,32},{32,36}... | collective-permute-start | bytes 393224 | tf_op jit(solution)/shard_map/while/body/eval_jaxpr/ppermute | solution.py:17
  257.1 9.6 %collective-permute-start = (bf16[2,32,8,128]{3,1,2,0:T(8,128)(2,1)S(1)}, bf16[2,32,8,128]{3,1,2,0:T(8,128)(2,1)S(1)}, u32[]{:S(2)}, u32[]{:S(2)}) collective-permute-start(bf16[2,32,8,128]{3,1,2,0:T(8,128)(2,1)S(1)} %get-tuple-element.334), channel_id=1, source_target_pairs={{0,4},{4,8},{8,12},{12,16},{16,20},{20,24},{24,28},{28,32},{32,36}... | collective-permute-start | bytes 393224 | tf_op jit(solution)/shard_map/while/body/eval_jaxpr/ppermute | solution.py:17
  267.2 9.6 %collective-permute-start = (bf16[2,32,8,128]{3,1,2,0:T(8,128)(2,1)S(1)}, bf16[2,32,8,128]{3,1,2,0:T(8,128)(2,1)S(1)}, u32[]{:S(2)}, u32[]{:S(2)}) collective-permute-start(bf16[2,32,8,128]{3,1,2,0:T(8,128)(2,1)S(1)} %get-tuple-element.334), channel_id=1, source_target_pairs={{0,4},{4,8},{8,12},{12,16},{16,20},{20,24},{24,28},{28,32},{32,36}... | collective-permute-start | bytes 393224 | tf_op jit(solution)/shard_map/while/body/eval_jaxpr/ppermute | solution.py:17
where the time goes:
time: 296 us; the launch traced here: 295 us
  blocking collectives  175 us (59%)
  waiting for transfers between devices  68 us (23%)
  starting transfers between devices  27.7 us (9%)
  matrix products  10.9 us (4%)
  local copies, waits for them, and re-layouts  8.66 us (3%)
  other arithmetic  4 us (1%)
    all_gather x1, blocking collectives, on_device(): lax.all_gather(far_k, 'ctx', axis=0, tiled=True)  85.1 us
    all_gather x1, blocking collectives, on_device(): lax.all_gather(far_v, 'ctx', axis=0, tiled=True)  80.7 us
    ppermute x8, waiting for transfers between devices, shifted(): return lax.ppermute(block, axis, route)  53 us
    ppermute x8, starting transfers between devices, shifted(): return lax.ppermute(block, axis, route)  16.6 us
    all_to_all x1, blocking collectives, on_device(): lax.all_to_all(merged, 'head', split_axis=0, concat_axis=1, tiled=True)  9.07 us
    all_to_all x1, waiting for transfers between devices, on_device(): lax.all_to_all(key_rows, 'head', split_axis=1, concat_axis=0, tiled=True)  6.57 us
    all_to_all x1, waiting for transfers between devices, on_device(): lax.all_to_all(value_rows, 'head', split_axis=1, concat_axis=0, tiled=True)  6.48 us
  transfers between devices with their start and end apart: 11, of which 10 were waited for; matrix products, arithmetic and copies ran while one was open for 4% of the time, Pallas kernels for 0%

commit v1 on v0

--- a/solution.py
+++ b/solution.py
@@ -3,6 +3,7 @@
 import jax.numpy as jnp
 from jax import lax
 from jax.sharding import PartitionSpec as P
+from jax.lax import all_to_all, axis_size
 
 DH = 128
 BUCKETS = 32
@@ -214,7 +215,15 @@
         start_state(far_rows, n_heads),
         far_q,
         lax.all_gather(far_k, "ctx", axis=0, tiled=True),
-        lax.all_gather(far_v, "ctx", axis=0, tiled=True),
+        jnp.concatenate(
+            all_to_all(
+                jnp.stack([far_v for _ in range(axis_size("ctx"))]),
+                concat_axis=0,
+                split_axis=0,
+                axis_name="ctx",
+            ),
+            axis=0,
+        ),
         place * far_rows,
         long_rate,
         rel_bias,

time: 296 us -> 248 us (0.84)
  blocking collectives: 175 us -> 94.2 us
  waiting for transfers between devices: 68 us -> 83.2 us
  starting transfers between devices: 27.7 us -> 42.1 us
  local copies, waits for them, and re-layouts: 8.66 us -> 11.7 us
    all_gather x1 -> x0, blocking collectives: 80.7 us -> none  [on_device(): lax.all_gather(far_v, 'ctx', axis=0, tiled=True)]
    ppermute x8, waiting for transfers between devices: 53 us -> 68.1 us  [shifted(): return lax.ppermute(block, axis, route)]
    all_to_all x0 -> x1, starting transfers between devices: none -> 13.8 us  [on_device(): all_to_all(jnp.stack([far_v for _ in range(axis_size('ctx'))]), concat_ax...]
  transfers between devices with their start and end apart: 11 -> 12, of which waited for: 10 -> 10; matrix products, arithmetic and copies ran while one was open for 4% -> 8% of each run, Pallas kernels for 0% -> 0%
where the time goes in v1:
time: 248 us; the launch traced here: 247 us
  blocking collectives  94.2 us (38%)
  waiting for transfers between devices  83.2 us (34%)
  starting transfers between devices  42.1 us (17%)
  local copies, waits for them, and re-layouts  11.7 us (5%)
  matrix products  10.9 us (4%)
  other arithmetic  3.79 us (2%)
    all_gather x1, blocking collectives, on_device(): lax.all_gather(far_k, 'ctx', axis=0, tiled=True)  85.1 us
    ppermute x8, waiting for transfers between devices, shifted(): return lax.ppermute(block, axis, route)  68.1 us
    ppermute x8, starting transfers between devices, shifted(): return lax.ppermute(block, axis, route)  17.1 us
    all_to_all x1, starting transfers between devices, on_device(): all_to_all(jnp.stack([far_v for _ in range(axis_size('ctx'))]), concat_ax...  13.8 us
    all_to_all x1, blocking collectives, on_device(): lax.all_to_all(merged, 'head', split_axis=0, concat_axis=1, tiled=True)  9.07 us
    all_to_all x1, waiting for transfers between devices, on_device(): lax.all_to_all(value_rows, 'head', split_axis=1, concat_axis=0, tiled=True)  6.63 us
    all_to_all x1, waiting for transfers between devices, on_device(): lax.all_to_all(key_rows, 'head', split_axis=1, concat_axis=0, tiled=True)  6.57 us
  transfers between devices with their start and end apart: 12, of which 10 were waited for; matrix products, arithmetic and copies ran while one was open for 8% of the time, Pallas kernels for 0%

profile of v1, /device:TPU:128, one launch (start us, length us, event | category | flops | bytes accessed | tf_op | source)
XLA Modules:
  0.0 247.1 jit_solution(13583375859164731686)
XLA Ops:
  0.0 1.7 copy.298
  1.7 4.4 %all-to-all-start = ((bf16[32,4,1024]{2,0,1:T(8,128)(2,1)}), bf16[32,4,1024]{2,0,1:T(8,128)(2,1)S(1)}, u32[]{:S(2)}, u32[]{:S(2)}) async-start(bf16[32,4,1024]{2,0,1:T(8,128)(2,1)} %bitcast.230), calls=%async_computation | async-start | bytes 524288 | tf_op jit(solution)/shard_map/all_to_all | solution.py:175
  6.9 0.7 copy.297
  7.6 0.7 copy.296
  8.4 0.7 fusion.31
  9.4 0.7 fusion.30
  10.2 0.2 copy.201
  10.4 0.3 fusion.51
  10.8 2.0 all-to-all-done
  12.8 3.4 %all-to-all-start.1 = ((bf16[32,4,1024]{2,0,1:T(8,128)(2,1)}), bf16[32,4,1024]{2,0,1:T(8,128)(2,1)S(1)}, u32[]{:S(2)}, u32[]{:S(2)}) async-start(bf16[32,4,1024]{2,0,1:T(8,128)(2,1)} %bitcast.229), calls=%async_computation.1 | async-start | bytes 524288 | tf_op jit(solution)/shard_map/all_to_all | solution.py:176
  16.3 6.6 %all-to-all-done.1 = bf16[32,4,1024]{2,0,1:T(8,128)(2,1)S(1)} async-done(((bf16[32,4,1024]{2,0,1:T(8,128)(2,1)}), bf16[32,4,1024]{2,0,1:T(8,128)(2,1)S(1)}, u32[]{:S(2)}, u32[]{:S(2)}) %all-to-all-start.1) | async-done | bytes 262176 | tf_op jit(solution)/shard_map/all_to_all | solution.py:176
  22.8 3.4 %all-to-all-start.2 = ((bf16[32,4,1024]{2,0,1:T(8,128)(2,1)}), bf16[32,4,1024]{2,0,1:T(8,128)(2,1)S(1)}, u32[]{:S(2)}, u32[]{:S(2)}) async-start(bf16[32,4,1024]{2,0,1:T(8,128)(2,1)} %bitcast.228), calls=%async_computation.2 | async-start | bytes 524288 | tf_op jit(solution)/shard_map/all_to_all | solution.py:177
  26.3 6.6 %all-to-all-done.2 = bf16[32,4,1024]{2,0,1:T(8,128)(2,1)S(1)} async-done(((bf16[32,4,1024]{2,0,1:T(8,128)(2,1)}), bf16[32,4,1024]{2,0,1:T(8,128)(2,1)S(1)}, u32[]{:S(2)}, u32[]{:S(2)}) %all-to-all-start.2) | async-done | bytes 262176 | tf_op jit(solution)/shard_map/all_to_all | solution.py:177
  32.9 0.2 fusion.58
  33.2 85.1 %all_gather.3 = bf16[256,8,128]{2,1,0:T(8,128)(2,1)S(1)} all-gather(bf16[2,8,128]{2,1,0:T(8,128)(2,1)S(1)} %reduce_sum.144), channel_id=1, replica_groups=mesh['ctx'=128,'head'=4] {'ctx'}, dimensions={0}, use_global_device_ids=true | all-gather | bytes 528384 | tf_op jit(solution)/shard_map/all_gather | solution.py:217
  118.3 0.3 fusion.179
  119.0 1.1 stack.14
  120.1 13.8 %all-to-all-start.3 = ((bf16[128,2,8,128]{3,1,2,0:T(2,128)(2,1)}), bf16[128,2,8,128]{3,1,2,0:T(2,128)(2,1)S(1)}, u32[]{:S(2)}, u32[]{:S(2)}) async-start(bf16[128,2,8,128]{3,1,2,0:T(2,128)(2,1)} %stack.14), calls=%async_computation.3 | async-start | bytes 1048576 | tf_op jit(solution)/shard_map/all_to_all | solution.py:219
  134.1 0.9 pad_maximum_fusion
  134.9 2.2 collective-permute-start.1
  137.2 0.3 select_reduce_fusion
  138.1 90.0 %while.4 = (s32[]{:T(128)}, f32[8,32]{1,0:T(8,128)S(1)}, f32[8,32]{1,0:T(8,128)S(1)}, f32[32,8,128]{2,0,1:T(8,128)S(1)}, bf16[2,32,8,128]{3,1,2,0:T(8,128)(2,1)S...) while((s32[]{:T(128)}, f32[8,32]{1,0:T(8,128)S(1)}, ...), condition=%wide.region_12.13_spmd, body=%wide.region_9.12_spmd.sunk | while | flops 7575332 | bytes 1713579 | solution.py:170
  138.1 3.4 %collective-permute-start = (bf16[2,32,8,128]{3,1,2,0:T(8,128)(2,1)S(1)}, bf16[2,32,8,128]{3,1,2,0:T(8,128)(2,1)S(1)}, u32[]{:S(2)}, u32[]{:S(2)}) collective-permute-start(bf16[2,32,8,128]{3,1,2,0:T(8,128)(2,1)S(1)} %get-tuple-element.334), channel_id=1, source_target_pairs={{0,4},{4,8},{8,12},{12,16},{16,20},{20,24},{24,28},{28,32},{32,36}... | collective-permute-start | bytes 393224 | tf_op jit(solution)/shard_map/while/body/eval_jaxpr/ppermute | solution.py:18
  141.5 0.3 fusion.194
  141.9 24.7 %collective-permute-done = bf16[2,32,8,128]{3,1,2,0:T(8,128)(2,1)S(1)} collective-permute-done((bf16[2,32,8,128]{3,1,2,0:T(8,128)(2,1)S(1)}, bf16[2,32,8,128]{3,1,2,0:T(8,128)(2,1)S(1)}, u32[]{:S(2)}, u32[]{:S(2)}) %collective-permute-start) | collective-permute-done | bytes 131104 | tf_op jit(solution)/shard_map/while/body/eval_jaxpr/ppermute | solution.py:18
  166.9 0.2 fusion.199
  167.2 1.9 collective-permute-start
  169.2 0.3 fusion.194
  169.6 7.2 %collective-permute-done = bf16[2,32,8,128]{3,1,2,0:T(8,128)(2,1)S(1)} collective-permute-done((bf16[2,32,8,128]{3,1,2,0:T(8,128)(2,1)S(1)}, bf16[2,32,8,128]{3,1,2,0:T(8,128)(2,1)S(1)}, u32[]{:S(2)}, u32[]{:S(2)}) %collective-permute-start) | collective-permute-done | bytes 131104 | tf_op jit(solution)/shard_map/while/body/eval_jaxpr/ppermute | solution.py:18
  177.1 0.2 fusion.199
  177.3 1.9 collective-permute-start
  179.3 0.3 fusion.194
  179.7 7.2 %collective-permute-done = bf16[2,32,8,128]{3,1,2,0:T(8,128)(2,1)S(1)} collective-permute-done((bf16[2,32,8,128]{3,1,2,0:T(8,128)(2,1)S(1)}, bf16[2,32,8,128]{3,1,2,0:T(8,128)(2,1)S(1)}, u32[]{:S(2)}, u32[]{:S(2)}) %collective-permute-start) | collective-permute-done | bytes 131104 | tf_op jit(solution)/shard_map/while/body/eval_jaxpr/ppermute | solution.py:18
  187.2 0.2 fusion.199
  187.5 1.9 collective-permute-start
  189.5 0.3 fusion.194
  189.9 7.2 %collective-permute-done = bf16[2,32,8,128]{3,1,2,0:T(8,128)(2,1)S(1)} collective-permute-done((bf16[2,32,8,128]{3,1,2,0:T(8,128)(2,1)S(1)}, bf16[2,32,8,128]{3,1,2,0:T(8,128)(2,1)S(1)}, u32[]{:S(2)}, u32[]{:S(2)}) %collective-permute-start) | collective-permute-done | bytes 131104 | tf_op jit(solution)/shard_map/while/body/eval_jaxpr/ppermute | solution.py:18
  197.4 0.2 fusion.199
  197.6 1.9 collective-permute-start
  199.6 0.3 fusion.194
  200.0 7.2 %collective-permute-done = bf16[2,32,8,128]{3,1,2,0:T(8,128)(2,1)S(1)} collective-permute-done((bf16[2,32,8,128]{3,1,2,0:T(8,128)(2,1)S(1)}, bf16[2,32,8,128]{3,1,2,0:T(8,128)(2,1)S(1)}, u32[]{:S(2)}, u32[]{:S(2)}) %collective-permute-start) | collective-permute-done | bytes 131104 | tf_op jit(solution)/shard_map/while/body/eval_jaxpr/ppermute | solution.py:18
  207.5 0.2 fusion.199
  207.8 1.9 collective-permute-start
  209.7 0.3 fusion.194
  210.1 7.2 %collective-permute-done = bf16[2,32,8,128]{3,1,2,0:T(8,128)(2,1)S(1)} collective-permute-done((bf16[2,32,8,128]{3,1,2,0:T(8,128)(2,1)S(1)}, bf16[2,32,8,128]{3,1,2,0:T(8,128)(2,1)S(1)}, u32[]{:S(2)}, u32[]{:S(2)}) %collective-permute-start) | collective-permute-done | bytes 131104 | tf_op jit(solution)/shard_map/while/body/eval_jaxpr/ppermute | solution.py:18
  217.7 0.2 fusion.199
  217.9 1.9 collective-permute-start
  219.9 0.3 fusion.194
  220.3 7.2 %collective-permute-done = bf16[2,32,8,128]{3,1,2,0:T(8,128)(2,1)S(1)} collective-permute-done((bf16[2,32,8,128]{3,1,2,0:T(8,128)(2,1)S(1)}, bf16[2,32,8,128]{3,1,2,0:T(8,128)(2,1)S(1)}, u32[]{:S(2)}, u32[]{:S(2)}) %collective-permute-start) | collective-permute-done | bytes 131104 | tf_op jit(solution)/shard_map/while/body/eval_jaxpr/ppermute | solution.py:18
  227.8 0.2 fusion.199
  228.5 0.3 fusion.178
  228.8 1.3 fusion.177
  230.4 0.5 fusion.33
  230.8 1.3 fusion.42
  232.1 0.3 copy.225
  233.5 0.9 mul.190
  234.6 0.9 mul.193
  235.5 0.4 copy.229
  235.9 0.3 copy-done.6
  236.2 0.2 fusion.135
  236.6 0.4 copy-done
  237.0 0.3 divide_convert_fusion
  237.3 9.1 %all_to_all.69 = bf16[4,32,1024]{2,1,0:T(8,128)(2,1)S(1)} all-to-all(bf16[4,32,1024]{2,1,0:T(8,128)(2,1)S(1)} %divide_convert_fusion), channel_id=1, replica_groups=mesh['ctx'=128,'head'=4] {'head'}, dimensions={0} | all-to-all | bytes 524288 | tf_op jit(solution)/shard_map/all_to_all | solution.py:246
  246.4 0.7 copy.243
  (157 shorter events, 7.1 us)
Async XLA Ops:
  0.0 6.4 %copy-start.9 = (s32[2,8]{1,0:T(2,128)S(1)}, s32[2,8]{1,0:T(2,128)}, u32[]{:S(2)}) copy-start(s32[2,8]{1,0:T(2,128)} %param.11) | copy-start | bytes 196
  1.7 5.2 %copy-start.3 = (bf16[32,4096]{1,0:T(8,128)(2,1)S(1)}, bf16[32,4096]{1,0:T(8,128)(2,1)}, u32[]{:S(2)}) copy-start(bf16[32,4096]{1,0:T(8,128)(2,1)} %param.8) | copy-start | bytes 786436
  1.7 11.1 %all-to-all-start = ((bf16[32,4,1024]{2,0,1:T(8,128)(2,1)}), bf16[32,4,1024]{2,0,1:T(8,128)(2,1)S(1)}, u32[]{:S(2)}, u32[]{:S(2)}) async-start(bf16[32,4,1024]{2,0,1:T(8,128)(2,1)} %bitcast.230), calls=%async_computation | async-start | bytes 524288 | tf_op jit(solution)/shard_map/all_to_all | solution.py:175
  6.3 1.3 copy-start.4
  6.8 1.4 copy-start.2
  12.8 10.1 %all-to-all-start.1 = ((bf16[32,4,1024]{2,0,1:T(8,128)(2,1)}), bf16[32,4,1024]{2,0,1:T(8,128)(2,1)S(1)}, u32[]{:S(2)}, u32[]{:S(2)}) async-start(bf16[32,4,1024]{2,0,1:T(8,128)(2,1)} %bitcast.229), calls=%async_computation.1 | async-start | bytes 524288 | tf_op jit(solution)/shard_map/all_to_all | solution.py:176
  16.3 102.4 %copy-start.7 = (pred[2,256]{1,0:T(4,128)(4,1)}, pred[2,256]{1,0:T(4,128)(4,1)S(1)}, u32[]{:S(2)}) copy-start(pred[2,256]{1,0:T(4,128)(4,1)S(1)} %iota_compare_fusion.15) | copy-start | bytes 1540
  22.8 10.1 %all-to-all-start.2 = ((bf16[32,4,1024]{2,0,1:T(8,128)(2,1)}), bf16[32,4,1024]{2,0,1:T(8,128)(2,1)S(1)}, u32[]{:S(2)}, u32[]{:S(2)}) async-start(bf16[32,4,1024]{2,0,1:T(8,128)(2,1)} %bitcast.228), calls=%async_computation.2 | async-start | bytes 524288 | tf_op jit(solution)/shard_map/all_to_all | solution.py:177
  118.6 1.5 copy-start.5
  120.1 115.4 %all-to-all-start.3 = ((bf16[128,2,8,128]{3,1,2,0:T(2,128)(2,1)}), bf16[128,2,8,128]{3,1,2,0:T(2,128)(2,1)S(1)}, u32[]{:S(2)}, u32[]{:S(2)}) async-start(bf16[128,2,8,128]{3,1,2,0:T(2,128)(2,1)} %stack.14), calls=%async_computation.3 | async-start | bytes 1048576 | tf_op jit(solution)/shard_map/all_to_all | solution.py:219
  134.9 93.9 %collective-permute-start.1 = (bf16[2,128,8,128]{3,1,2,0:T(8,128)(2,1)}, bf16[2,128,8,128]{3,1,2,0:T(8,128)(2,1)}, u32[]{:S(2)}, u32[]{:S(2)}) collective-permute-start(bf16[2,128,8,128]{3,1,2,0:T(8,128)(2,1)} %pad_maximum_fusion), channel_id=1, source_target_pairs={{0,4},{4,8},{8,12},{12,16},{16,20},{20,24},{24,28},{28,32},{32,36}... | collective-permute-start | bytes 1572872 | tf_op jit(solution)/shard_map/while/body/eval_jaxpr/ppermute | solution.py:18
  138.1 28.6 %collective-permute-start = (bf16[2,32,8,128]{3,1,2,0:T(8,128)(2,1)S(1)}, bf16[2,32,8,128]{3,1,2,0:T(8,128)(2,1)S(1)}, u32[]{:S(2)}, u32[]{:S(2)}) collective-permute-start(bf16[2,32,8,128]{3,1,2,0:T(8,128)(2,1)S(1)} %get-tuple-element.334), channel_id=1, source_target_pairs={{0,4},{4,8},{8,12},{12,16},{16,20},{20,24},{24,28},{28,32},{32,36}... | collective-permute-start | bytes 393224 | tf_op jit(solution)/shard_map/while/body/eval_jaxpr/ppermute | solution.py:18
  167.2 9.6 %collective-permute-start = (bf16[2,32,8,128]{3,1,2,0:T(8,128)(2,1)S(1)}, bf16[2,32,8,128]{3,1,2,0:T(8,128)(2,1)S(1)}, u32[]{:S(2)}, u32[]{:S(2)}) collective-permute-start(bf16[2,32,8,128]{3,1,2,0:T(8,128)(2,1)S(1)} %get-tuple-element.334), channel_id=1, source_target_pairs={{0,4},{4,8},{8,12},{12,16},{16,20},{20,24},{24,28},{28,32},{32,36}... | collective-permute-start | bytes 393224 | tf_op jit(solution)/shard_map/while/body/eval_jaxpr/ppermute | solution.py:18
  177.3 9.6 %collective-permute-start = (bf16[2,32,8,128]{3,1,2,0:T(8,128)(2,1)S(1)}, bf16[2,32,8,128]{3,1,2,0:T(8,128)(2,1)S(1)}, u32[]{:S(2)}, u32[]{:S(2)}) collective-permute-start(bf16[2,32,8,128]{3,1,2,0:T(8,128)(2,1)S(1)} %get-tuple-element.334), channel_id=1, source_target_pairs={{0,4},{4,8},{8,12},{12,16},{16,20},{20,24},{24,28},{28,32},{32,36}... | collective-permute-start | bytes 393224 | tf_op jit(solution)/shard_map/while/body/eval_jaxpr/ppermute | solution.py:18
  187.5 9.6 %collective-permute-start = (bf16[2,32,8,128]{3,1,2,0:T(8,128)(2,1)S(1)}, bf16[2,32,8,128]{3,1,2,0:T(8,128)(2,1)S(1)}, u32[]{:S(2)}, u32[]{:S(2)}) collective-permute-start(bf16[2,32,8,128]{3,1,2,0:T(8,128)(2,1)S(1)} %get-tuple-element.334), channel_id=1, source_target_pairs={{0,4},{4,8},{8,12},{12,16},{16,20},{20,24},{24,28},{28,32},{32,36}... | collective-permute-start | bytes 393224 | tf_op jit(solution)/shard_map/while/body/eval_jaxpr/ppermute | solution.py:18
  197.6 9.6 %collective-permute-start = (bf16[2,32,8,128]{3,1,2,0:T(8,128)(2,1)S(1)}, bf16[2,32,8,128]{3,1,2,0:T(8,128)(2,1)S(1)}, u32[]{:S(2)}, u32[]{:S(2)}) collective-permute-start(bf16[2,32,8,128]{3,1,2,0:T(8,128)(2,1)S(1)} %get-tuple-element.334), channel_id=1, source_target_pairs={{0,4},{4,8},{8,12},{12,16},{16,20},{20,24},{24,28},{28,32},{32,36}... | collective-permute-start | bytes 393224 | tf_op jit(solution)/shard_map/while/body/eval_jaxpr/ppermute | solution.py:18
  207.8 9.6 %collective-permute-start = (bf16[2,32,8,128]{3,1,2,0:T(8,128)(2,1)S(1)}, bf16[2,32,8,128]{3,1,2,0:T(8,128)(2,1)S(1)}, u32[]{:S(2)}, u32[]{:S(2)}) collective-permute-start(bf16[2,32,8,128]{3,1,2,0:T(8,128)(2,1)S(1)} %get-tuple-element.334), channel_id=1, source_target_pairs={{0,4},{4,8},{8,12},{12,16},{16,20},{20,24},{24,28},{28,32},{32,36}... | collective-permute-start | bytes 393224 | tf_op jit(solution)/shard_map/while/body/eval_jaxpr/ppermute | solution.py:18
  217.9 9.6 %collective-permute-start = (bf16[2,32,8,128]{3,1,2,0:T(8,128)(2,1)S(1)}, bf16[2,32,8,128]{3,1,2,0:T(8,128)(2,1)S(1)}, u32[]{:S(2)}, u32[]{:S(2)}) collective-permute-start(bf16[2,32,8,128]{3,1,2,0:T(8,128)(2,1)S(1)} %get-tuple-element.334), channel_id=1, source_target_pairs={{0,4},{4,8},{8,12},{12,16},{16,20},{20,24},{24,28},{28,32},{32,36}... | collective-permute-start | bytes 393224 | tf_op jit(solution)/shard_map/while/body/eval_jaxpr/ppermute | solution.py:18
  235.5 0.7 copy-start.6
  235.5 0.7 copy-start.8
  235.5 1.1 copy-start.1
  235.9 1.1 copy-start
